TPU v7x, 128 devices: a whole 4x4x4 slice. The times are simulated.
128 devices in a mesh: grp: 4 (over y), dev: 32 (over x, z, core).
Axes of the slice: x: 4, y: 4, z: 4, core: 2. Of those that a mesh axis runs over, the one named last changes fastest.
Arguments:
- points: bfloat16 [16384, 1024], P(('grp', 'dev')), may hold values from -6 to 6
- basis: bfloat16 [16384, 4096], P(('grp', 'dev')), may hold values from -0.75 to 0.75
- transfer_leaf: bfloat16 [16384, 4096], P(('grp', 'dev')), may hold values from -0.25 to 0.25
- transfer_mid: bfloat16 [2048, 4096], P(('grp', 'dev')), may hold values from -0.25 to 0.25
- near_blocks: bfloat16 [16384, 8, 4096], P(('grp', 'dev')), may hold values from -0.25 to 0.25
- near_src: int32 [16384, 8], P(('grp', 'dev')), may hold values from 0 to 16383, as said below
- leaf_coupling: bfloat16 [16384, 8, 4096], P(('grp', 'dev')), may hold values from -0.25 to 0.25
- far_leaf: int32 [16384, 8], P(('grp', 'dev')), may hold values from 0 to 16383, as said below
- mid_coupling: bfloat16 [2048, 16, 4096], P(('grp', 'dev')), may hold values from -0.1875 to 0.1875
- mid_target: int32 [2048, 16], P(('grp', 'dev')), may hold values from 0 to 2047, as said below
- top_coupling: bfloat16 [256, 16, 4096], P(('grp', 'dev')), may hold values from -0.1875 to 0.1875
- far_top: int32 [256, 16], P(('grp', 'dev')), may hold values from 0 to 255
Outputs:
- product: bfloat16 [16384, 1024], P(('grp', 'dev'))
Inputs may be any that keep to these rules, and one draw needn't show every extreme that they name: `near_src`: each row i names leaves at most 128 away from i; the first entry is i itself, and the first leaf of every device block but the first names the leaf 128 before it. `far_leaf`: each row i names leaves at most 128 away from i; the first leaf of every device block but the first names the leaf 128 before it. `mid_target`: among the entries of one device's 16 rows, at most 4 name clusters of any one aligned block of 16 clusters; one such block receives exactly 4 from every device's rows.
All inputs are finite; a program needn't handle non-finite values.
Results may differ from a plain program's by a relative error of at most 0.0065.
Values may be sent and summed in bfloat16 or wider, within the bound.
A program may use at most 192 MiB of HBM per device.

v0:
```python
import jax
import jax.numpy as jnp
from jax import lax
from jax.sharding import PartitionSpec as P

LEAF = 64
RANK = 64
RHS = 16
NEAR = 8
FAR_LEAF = 8
FAR_MID = 16
FAR_TOP = 16


def extended_2(array, sides, width):
    for axis, dim in sides:
        size, length = (lax.axis_size(axis), array.shape[dim])
        up = [(i, (i + 1) % size) for i in range(size - 1)]
        down = [(j, i) for i, j in up]
        last = lax.slice_in_dim(array, length - width, length, axis=dim)
        initial = lax.slice_in_dim(array, 0, width, axis=dim)
        before = lax.ppermute(last, axis, up)
        after = lax.ppermute(initial, axis, down)
        array = jnp.concatenate([before, array, after], axis=dim)
    return array


def body(
    points,
    basis,
    transfer_leaf,
    transfer_mid,
    near_blocks,
    near_src,
    leaf_coupling,
    far_leaf,
    mid_coupling,
    mid_target,
    top_coupling,
    far_top,
):
    f32 = jnp.float32
    bf = jnp.bfloat16
    nleaf = basis.shape[0]
    nmid = transfer_mid.shape[0]
    ntop = top_coupling.shape[0]
    width = RHS * RANK
    anchor = (lax.axis_index(("grp", "dev")) - 1) * nleaf
    extended = extended_2(points, ((("grp", "dev"), 0),), nleaf)
    near_picked = jnp.take(extended, near_src.reshape(-1) - anchor, axis=0).reshape(
        nleaf, NEAR, RHS, LEAF
    )
    near_out = jnp.einsum(
        "ijru,ijpu->irp",
        near_picked,
        near_blocks.reshape(nleaf, NEAR, LEAF, LEAF),
        preferred_element_type=f32,
    )
    vecs = basis.reshape(nleaf, LEAF, RANK)
    leaf_coef = jnp.einsum(
        "irp,ipk->irk", points.reshape(nleaf, RHS, LEAF), vecs, preferred_element_type=f32
    ).astype(bf)
    tleaf = transfer_leaf.reshape(nmid, 8, RANK, RANK)
    mid_coef = jnp.einsum(
        "qcrk,qckm->qrm", leaf_coef.reshape(nmid, 8, RHS, RANK), tleaf, preferred_element_type=f32
    ).astype(bf)
    tmid = transfer_mid.reshape(ntop, 8, RANK, RANK)
    top_coef = jnp.einsum(
        "tcrm,tcmn->trn", mid_coef.reshape(ntop, 8, RHS, RANK), tmid, preferred_element_type=f32
    ).astype(bf)
    contrib = jnp.einsum(
        "srb,sjab->sjra",
        mid_coef,
        mid_coupling.reshape(nmid, FAR_MID, RANK, RANK),
        preferred_element_type=f32,
    ).astype(bf)
    contrib = contrib.reshape(nmid * FAR_MID, width)
    targets = mid_target.reshape(-1)
    devices = lax.axis_size(("grp", "dev"))
    pairs = targets.shape[0]
    capacity = 2 * pairs // devices
    owner = targets // nmid
    local = targets % nmid
    onehot = (owner[:, None] == jnp.arange(devices, dtype=jnp.int32)[None, :]).astype(jnp.int32)
    earlier = jnp.sum((jnp.cumsum(onehot, axis=0) - onehot) * onehot, axis=1)
    position = owner * capacity + earlier
    outgoing = jnp.zeros((devices * capacity, width), bf).at[position].set(contrib)
    labels = jnp.full((devices * capacity,), -1, jnp.int32).at[position].set(local)
    arrived, arrived_labels = (
        lax.all_to_all(
            outgoing.reshape(devices, capacity, width),
            ("grp", "dev"),
            split_axis=0,
            concat_axis=0,
            tiled=True,
        ),
        lax.all_to_all(
            labels.reshape(devices, capacity),
            ("grp", "dev"),
            split_axis=0,
            concat_axis=0,
            tiled=True,
        ),
    )
    select = (arrived_labels.reshape(1, -1) == jnp.arange(nmid, dtype=jnp.int32)[:, None]).astype(
        bf
    )
    mid_far = jnp.dot(select, arrived.reshape(-1, width), preferred_element_type=f32)
    ext_coef = extended_2(leaf_coef.reshape(nleaf, width), ((("grp", "dev"), 0),), nleaf)
    leaf_picked = jnp.take(ext_coef, far_leaf.reshape(-1) - anchor, axis=0).reshape(
        nleaf, FAR_LEAF, RHS, RANK
    )
    leaf_far = jnp.einsum(
        "ijrb,ijab->ira",
        leaf_picked,
        leaf_coupling.reshape(nleaf, FAR_LEAF, RANK, RANK),
        preferred_element_type=f32,
    )
    all_top = lax.all_gather(top_coef.reshape(ntop, width), ("grp", "dev"), axis=0, tiled=True)
    top_picked = jnp.take(all_top, far_top.reshape(-1), axis=0).reshape(ntop, FAR_TOP, RHS, RANK)
    top_far = jnp.einsum(
        "tjrb,tjab->tra",
        top_picked,
        top_coupling.reshape(ntop, FAR_TOP, RANK, RANK),
        preferred_element_type=f32,
    )
    top_field = top_far.astype(bf)
    down_mid = jnp.einsum("trn,tcmn->tcrm", top_field, tmid, preferred_element_type=f32).reshape(
        nmid, RHS, RANK
    )
    mid_field = (mid_far.reshape(nmid, RHS, RANK) + down_mid).astype(bf)
    down_leaf = jnp.einsum("qrm,qckm->qcrk", mid_field, tleaf, preferred_element_type=f32).reshape(
        nleaf, RHS, RANK
    )
    leaf_field = (leaf_far + down_leaf).astype(bf)
    far_out = jnp.einsum("irk,ipk->irp", leaf_field, vecs, preferred_element_type=f32)
    return (near_out + far_out).reshape(nleaf, RHS * LEAF).astype(bf)


def solution(mesh):
    return jax.shard_map(
        body,
        mesh=mesh,
        in_specs=(
            P(("grp", "dev"), None),
            P(("grp", "dev"), None),
            P(("grp", "dev"), None),
            P(("grp", "dev"), None),
            P(("grp", "dev"), None, None),
            P(("grp", "dev"), None),
            P(("grp", "dev"), None, None),
            P(("grp", "dev"), None),
            P(("grp", "dev"), None, None),
            P(("grp", "dev"), None),
            P(("grp", "dev"), None, None),
            P(("grp", "dev"), None),
        ),
        out_specs=P(("grp", "dev"), None),
        check_vma=False,
    )
```

profile of v0, /device:TPU:0, one launch (start us, length us, event | category | flops | bytes accessed | tf_op | source)
XLA Modules:
  0.0 250.1 jit_solution(3562085039304243362)
XLA Ops:
  0.0 2.3 copy.59
  2.3 4.0 %copy.61 = bf16[128,64,64]{2,1,0:T(8,128)(2,1)S(1)} copy(bf16[128,64,64]{0,2,1:T(8,128)(2,1)} %bitcast.110) | data formatting | bytes 2097152 | tf_op jit(solution)/shard_map/reshape | solution.py:59
  12.2 5.3 %collective-permute-start = (bf16[128,1024]{1,0:T(8,128)(2,1)}, bf16[128,1024]{1,0:T(8,128)(2,1)}, u32[]{:S(2)}, u32[]{:S(2)}) collective-permute-start(bf16[128,1024]{1,0:T(8,128)(2,1)} %param.14), channel_id=1, source_target_pairs={{0,1},{1,2},{2,3},{3,4},{4,5},{5,6},{6,7},{7,8},{8,9},{9,10},{10,1... | collective-permute-start | bytes 786440 | tf_op jit(solution)/shard_map/ppermute | solution.py:22
  21.8 15.0 %all-to-all-start = ((s32[128,1,4]{2,1,0:T(1,128)}), s32[128,1,4]{2,1,0:T(1,128)S(1)}, u32[]{:S(2)}, u32[]{:S(2)}) async-start(s32[128,1,4]{2,1,0:T(1,128)} %bitcast.14), calls=%async_computation | async-start | bytes 131072 | tf_op jit(solution)/shard_map/all_to_all | solution.py:97
  37.1 4.3 %reshape.259 = bf16[16,8,64,64]{3,2,1,0:T(8,128)(2,1)} reshape(bf16[128,4096]{1,0:T(8,128)(2,1)} %param.16) | data formatting | bytes 2097152 | tf_op jit(solution)/shard_map/reshape | solution.py:63
  41.4 6.9 %reshape.260 = bf16[16,16,64,64]{3,2,1,0:T(8,128)(2,1)} reshape(bf16[16,16,4096]{2,1,0:T(8,128)(2,1)} %param.22) | data formatting | bytes 4194304 | tf_op jit(solution)/shard_map/reshape | solution.py:74
  50.6 6.5 %fusion = bf16[16,16,16,64]{3,2,1,0:T(8,128)(2,1)} fusion(bf16[16,16,64,64]{3,2,1,0:T(8,128)(2,1)} %reshape.260, bf16[16,16,64]{2,1,0:T(8,128)(2,1)S(1)} %fusion.7), kind=kOutput, calls=%fused_computation.8 | convolution fusion | flops 33816576 | bytes 2654208 | tf_op jit(solution)/shard_map/srb,sjab->sjra/dot_general | solution.py:71
  57.4 36.8 %all-gather = bf16[128,2,1024]{2,1,0:T(2,128)(2,1)S(1)} all-gather(bf16[1,2,1024]{2,1,0:T(2,128)(2,1)S(1)} %reshape.313), channel_id=1, replica_groups=mesh['grp'=4,'dev'=32] {'grp','dev'}, dimensions={0}, use_global_device_ids=true | all-gather | bytes 528384 | tf_op jit(solution)/shard_map/all_gather | solution.py:119
  99.4 2.7 %scatter_custom_fusion.1 = bf16[512,1024]{1,0:T(8,128)(2,1)} fusion(s32[256]{0:T(256)S(1)} %bitcast.122, bf16[256,1024]{1,0:T(8,128)(2,1)S(1)} %reshape.307, bf16[]{:T(256)} %constant.76.clone.1), kind=kCustom, calls=%fused_computation.30 | custom fusion | bytes 1048578 | tf_op jit(solution)/shard_map/scatter | solution.py:87
  104.3 12.5 %copy.66 = bf16[128,8,4096]{0,2,1:T(8,128)(2,1)} copy(bf16[128,8,4096]{2,1,0:T(8,128)(2,1)} %param.20) | data formatting | bytes 16777216 | tf_op args[6]
  116.8 24.0 %copy.67 = bf16[128,8,64,64]{3,2,1,0:T(8,128)(2,1)} copy(bf16[128,8,64,64]{0,3,2,1:T(8,128)(2,1)} %bitcast.106) | data formatting | bytes 16777216 | tf_op jit(solution)/shard_map/reshape | solution.py:116
  140.7 12.5 %copy.55 = bf16[128,8,4096]{0,2,1:T(8,128)(2,1)} copy(bf16[128,8,4096]{2,1,0:T(8,128)(2,1)} %param.18) | data formatting | bytes 16777216 | tf_op args[4]
  153.2 24.0 %copy.56 = bf16[128,8,64,64]{3,2,1,0:T(8,128)(2,1)} copy(bf16[128,8,64,64]{0,3,2,1:T(8,128)(2,1)} %bitcast.107) | data formatting | bytes 16777216 | tf_op jit(solution)/shard_map/reshape | solution.py:56
  177.2 6.9 %all-to-all-start.1 = ((bf16[128,4,1024]{2,1,0:T(4,128)(2,1)}), bf16[128,4,1024]{2,1,0:T(4,128)(2,1)}, u32[]{:S(2)}, u32[]{:S(2)}) async-start(bf16[128,4,1024]{2,1,0:T(4,128)(2,1)} %reshape.262), calls=%async_computation.1 | async-start | bytes 2097152 | tf_op jit(solution)/shard_map/all_to_all | solution.py:90
  186.8 5.4 %gather_fusion.2 = bf16[1024,1024]{1,0:T(8,128)(2,1)} fusion(bf16[384,1024]{1,0:T(8,128)(2,1)S(1)} %pad_maximum_fusion.1, s32[1024]{0:T(1024)S(1)} %fusion.32), kind=kCustom, calls=%fused_computation.1.clone | custom fusion | bytes 4198400 | tf_op jit(solution)/shard_map/jit(_take)/gather | solution.py:110
  192.1 3.2 %broadcast_select_fusion = bf16[1024,1024]{1,0:T(8,128)(2,1)} fusion(bf16[1024,1024]{1,0:T(8,128)(2,1)} %gather_fusion.2, pred[1024]{0:T(1024)(128)(4,1)S(1)} %compare_and_fusion), kind=kLoop, calls=%fused_computation.5 | loop fusion | flops 1048576 | bytes 4195328 | tf_op jit(solution)/shard_map/jit(_take)/select_n | solution.py:110
  195.3 6.4 %reshape.252 = bf16[128,8,16,64]{3,2,1,0:T(8,128)(2,1)} reshape(bf16[1024,1024]{1,0:T(8,128)(2,1)} %broadcast_select_fusion) | data formatting | bytes 4194304 | tf_op jit(solution)/shard_map/reshape | solution.py:110
  202.8 5.4 %gather_fusion.1 = bf16[1024,1024]{1,0:T(8,128)(2,1)} fusion(bf16[384,1024]{1,0:T(8,128)(2,1)S(1)} %pad_maximum_fusion, s32[1024]{0:T(1024)S(1)} %fusion.31), kind=kCustom, calls=%fused_computation.clone | custom fusion | bytes 4198400 | tf_op jit(solution)/shard_map/jit(_take)/gather | solution.py:50
  208.2 3.1 %broadcast_select_fusion.1 = bf16[1024,1024]{1,0:T(8,128)(2,1)} fusion(bf16[1024,1024]{1,0:T(8,128)(2,1)} %gather_fusion.1, pred[1024]{0:T(1024)(128)(4,1)S(1)} %compare_and_fusion.1), kind=kLoop, calls=%fused_computation.6 | loop fusion | flops 1048576 | bytes 4195328 | tf_op jit(solution)/shard_map/jit(_take)/select_n | solution.py:50
  211.3 6.4 %reshape.247 = bf16[128,8,16,64]{3,2,1,0:T(8,128)(2,1)} reshape(bf16[1024,1024]{1,0:T(8,128)(2,1)} %broadcast_select_fusion.1) | data formatting | bytes 4194304 | tf_op jit(solution)/shard_map/reshape | solution.py:50
  219.9 2.3 copy.71
  223.9 4.3 %fusion.23 = f32[16,16,8,64]{3,1,2,0:T(8,128)} fusion(bf16[16,8,64,64]{3,2,1,0:T(8,128)(2,1)} %reshape.259, bf16[16,16,64,1]{2,0,1,3:T(8,128)(2,1)S(1)} %fusion.8), kind=kOutput, calls=%fused_computation.42 | convolution fusion | flops 16777216 | bytes 1605632 | tf_op jit(solution)/shard_map/qrm,qckm->qcrk/dot_general | solution.py:132
  228.2 10.8 %fusion.5 = f32[128,16,64]{2,1,0:T(8,128)} fusion(bf16[128,64,64]{2,1,0:T(8,128)(2,1)S(1)} %copy.61, f32[128,16,64]{2,1,0:T(8,128)} %bitcast.109, bf16[128,8,16,64]{3,2,1,0:T(8,128)(2,1)} %reshape.252, bf16[128,8,64,64]{3,2,1,0:T(8,128)(2,1)} %copy.67), kind=kOutput, calls=%fused_computation.16 | convolution fusion | flops 151257088 | bytes 12582912 | tf_op jit(solution)/shard_map/irk,ipk->irp/dot_general | solution.py:136
  239.0 9.7 %fusion.3 = bf16[128,16,64]{2,1,0:T(8,128)(2,1)S(1)} fusion(f32[128,16,64]{2,1,0:T(8,128)} %fusion.5, bf16[128,8,16,64]{3,2,1,0:T(8,128)(2,1)} %reshape.247, bf16[128,8,64,64]{3,2,1,0:T(8,128)(2,1)} %copy.56), kind=kOutput, calls=%fused_computation.13 | convolution fusion | flops 134479872 | bytes 11272192 | tf_op jit(solution)/shard_map/ijru,ijpu->irp/dot_general | solution.py:53
  (78 shorter events, 29.3 us)
Async XLA Ops:
  2.3 4.0 %copy-start = (bf16[128,1024]{1,0:T(8,128)(2,1)S(1)}, bf16[128,1024]{1,0:T(8,128)(2,1)}, u32[]{:S(2)}) copy-start(bf16[128,1024]{1,0:T(8,128)(2,1)} %param.14) | copy-start | bytes 786436
  6.9 11.9 %copy-start.3 = (s32[16,16]{1,0:T(8,128)S(1)}, s32[16,16]{1,0:T(8,128)}, u32[]{:S(2)}) copy-start(s32[16,16]{1,0:T(8,128)} %param.23) | copy-start | bytes 3076
  6.9 29.9 %copy-start.6 = (s32[2,16]{1,0:T(2,128)S(1)}, s32[2,16]{1,0:T(2,128)}, u32[]{:S(2)}) copy-start(s32[2,16]{1,0:T(2,128)} %param.25) | copy-start | bytes 388
  6.9 30.0 %copy-start.4 = (s32[128,8]{0,1:T(8,128)S(1)}, s32[128,8]{0,1:T(8,128)}, u32[]{:S(2)}) copy-start(s32[128,8]{0,1:T(8,128)} %param.21) | copy-start | bytes 12292
  6.9 30.0 %copy-start.5 = (s32[128,8]{0,1:T(8,128)S(1)}, s32[128,8]{0,1:T(8,128)}, u32[]{:S(2)}) copy-start(s32[128,8]{0,1:T(8,128)} %param.19) | copy-start | bytes 12292
  8.9 176.7 %collective-permute-start.2 = (bf16[128,1024]{1,0:T(8,128)(2,1)}, bf16[128,1024]{1,0:T(8,128)(2,1)}, u32[]{:S(2)}, u32[]{:S(2)}) collective-permute-start(bf16[128,1024]{1,0:T(8,128)(2,1)} %copy.63), channel_id=1, source_target_pairs={{0,1},{1,2},{2,3},{3,4},{4,5},{5,6},{6,7},{7,8},{8,9},{9,10},{10,1... | collective-permute-start | bytes 786440 | tf_op jit(solution)/shard_map/ppermute | solution.py:22
  10.9 174.7 %collective-permute-start.3 = (bf16[128,1024]{1,0:T(8,128)(2,1)}, bf16[128,1024]{1,0:T(8,128)(2,1)}, u32[]{:S(2)}, u32[]{:S(2)}) collective-permute-start(bf16[128,1024]{1,0:T(8,128)(2,1)} %copy.63), channel_id=1, source_target_pairs={{1,0},{2,1},{3,2},{4,3},{5,4},{6,5},{7,6},{8,7},{9,8},{10,9},{11,1... | collective-permute-start | bytes 786440 | tf_op jit(solution)/shard_map/ppermute | solution.py:23
  12.2 189.6 %collective-permute-start = (bf16[128,1024]{1,0:T(8,128)(2,1)}, bf16[128,1024]{1,0:T(8,128)(2,1)}, u32[]{:S(2)}, u32[]{:S(2)}) collective-permute-start(bf16[128,1024]{1,0:T(8,128)(2,1)} %param.14), channel_id=1, source_target_pairs={{0,1},{1,2},{2,3},{3,4},{4,5},{5,6},{6,7},{7,8},{8,9},{9,10},{10,1... | collective-permute-start | bytes 786440 | tf_op jit(solution)/shard_map/ppermute | solution.py:22
  17.5 184.3 %collective-permute-start.1 = (bf16[128,1024]{1,0:T(8,128)(2,1)}, bf16[128,1024]{1,0:T(8,128)(2,1)}, u32[]{:S(2)}, u32[]{:S(2)}) collective-permute-start(bf16[128,1024]{1,0:T(8,128)(2,1)} %param.14), channel_id=1, source_target_pairs={{1,0},{2,1},{3,2},{4,3},{5,4},{6,5},{7,6},{8,7},{9,8},{10,9},{11,1... | collective-permute-start | bytes 786440 | tf_op jit(solution)/shard_map/ppermute | solution.py:23
  21.8 155.4 %all-to-all-start = ((s32[128,1,4]{2,1,0:T(1,128)}), s32[128,1,4]{2,1,0:T(1,128)S(1)}, u32[]{:S(2)}, u32[]{:S(2)}) async-start(s32[128,1,4]{2,1,0:T(1,128)} %bitcast.14), calls=%async_computation | async-start | bytes 131072 | tf_op jit(solution)/shard_map/all_to_all | solution.py:97
  41.3 6.9 %copy-start.2 = (bf16[16,4096]{1,0:T(8,128)(2,1)S(1)}, bf16[16,4096]{1,0:T(8,128)(2,1)}, u32[]{:S(2)}) copy-start(bf16[16,4096]{1,0:T(8,128)(2,1)} %param.17) | copy-start | bytes 393220
  177.2 40.5 %all-to-all-start.1 = ((bf16[128,4,1024]{2,1,0:T(4,128)(2,1)}), bf16[128,4,1024]{2,1,0:T(4,128)(2,1)}, u32[]{:S(2)}, u32[]{:S(2)}) async-start(bf16[128,4,1024]{2,1,0:T(4,128)(2,1)} %reshape.262), calls=%async_computation.1 | async-start | bytes 2097152 | tf_op jit(solution)/shard_map/all_to_all | solution.py:90
  195.3 6.5 %copy-start.1 = (bf16[128,1024]{1,0:T(8,128)(2,1)S(1)}, bf16[128,1024]{1,0:T(8,128)(2,1)}, u32[]{:S(2)}) copy-start(bf16[128,1024]{1,0:T(8,128)(2,1)} %param.14) | copy-start | bytes 786436
where the time goes:
time: 253 us; the launch traced here: 250 us
  local copies, waits for them, and re-layouts  135 us (53%)
  blocking collectives  36.8 us (15%)
  matrix products  36.6 us (14%)
  starting transfers between devices  31.7 us (13%)
  other arithmetic  9.87 us (4%)
    all_gather x1, blocking collectives, body(): lax.all_gather(top_coef.reshape(ntop, width), ('grp', 'dev'), axis=0, til...  36.8 us
    unnamed x21, local copies, waits for them, and re-layouts  27.7 us
    reshape x1, local copies, waits for them, and re-layouts, body(): near_blocks.reshape(nleaf, NEAR, LEAF, LEAF)  24 us
    reshape x1, local copies, waits for them, and re-layouts, body(): leaf_coupling.reshape(nleaf, FAR_LEAF, RANK, RANK)  24 us
    all_to_all x1, starting transfers between devices, body(): lax.all_to_all(labels.reshape(devices, capacity), ('grp', 'dev'), split_a...  15 us
    dot_general x1, matrix products, body(): jnp.einsum('irk,ipk->irp', leaf_field, vecs, preferred_element_type=f32)  10.8 us
    dot_general x1, matrix products, body(): jnp.einsum('ijru,ijpu->irp', near_picked, near_blocks.reshape(nleaf, NEAR...  9.74 us
    ppermute x2, starting transfers between devices, extended_2(): before = lax.ppermute(last, axis, up)  7.27 us
  transfers between devices with their start and end apart: 6, of which 0 were waited for; matrix products, arithmetic and copies ran while one was open for 56% of the time, Pallas kernels for 0%

commit v1 on v0

v1 whole, which is shorter than its diff:
```python
import functools

import jax
import jax.numpy as jnp
from jax import lax
from jax.experimental import pallas as pl
from jax.experimental.pallas import tpu as pltpu
from jax.sharding import PartitionSpec as P

F32 = jnp.float32
BF = jnp.bfloat16
AXES = ("grp", "dev")
GROUPS = 16
DEVICES = 128
LEAVES = 16
STEPS = 128 // LEAVES


def dot(a, b):
    return jnp.dot(a, b, preferred_element_type=F32)


def dot_nt(a, b):
    return lax.dot_general(a, b, (((1,), (1,)), ((), ())), preferred_element_type=F32)


def iota(shape, dim):
    return lax.broadcasted_iota(jnp.int32, shape, dim)


def ones_where(condition):
    return jnp.where(condition, 1.0, 0.0).astype(BF)


def low_lanes(shape):
    return iota(shape, len(shape) - 1) < 64


def spread(half):
    shape = (64, 256)
    return ones_where(iota(shape, 0) == 2 * (iota(shape, 1) // 8) + half)


def gather_back(half):
    shape = (128, 256)
    return ones_where(iota(shape, 0) % 64 == 2 * (iota(shape, 1) // 8) + half)


def own_child():
    shape = (128, 256)
    return iota(shape, 0) // 16 == iota(shape, 1) % 8


def fold_halves(first, second):
    v = jnp.where(low_lanes(first.shape), first, second)
    return v + pltpu.roll(v, 64, 1)


def both_halves(v):
    low = low_lanes(v.shape)
    zero = jnp.zeros_like(v)
    return jnp.concatenate([jnp.where(low, v, zero), jnp.where(low, zero, v)], axis=0)


def spread_sources(dst, n, v):
    low = low_lanes(v.shape)
    zero = jnp.zeros_like(v)
    count = v.shape[0] // 16
    dst[n : n + count, 0:16, :] = jnp.where(low, v, zero).reshape(count, 16, 128)
    dst[n : n + count, 16:32, :] = jnp.where(low, zero, v).reshape(count, 16, 128)


def up_pass(loads, points_ready, coefs_ready, pt, basis, tl, tm, xp, cp, mc, tops, xd, cd):
    e01 = jnp.concatenate([spread(0), spread(1)], axis=1)
    shape = (2048, 512)
    own = (iota(shape, 0) // 16) % 8 == iota(shape, 1) % 8
    shape = (128, 64)
    pick = ones_where(
        (iota(shape, 0) // 16 == iota(shape, 1) % 8)
        & ((iota(shape, 0) % 16) // 2 == iota(shape, 1) // 8)
    )
    shape = (128, 128)
    fold = ones_where(iota(shape, 0) % 64 == iota(shape, 1) % 64)
    parity = iota(shape, 1) // 64 == iota(shape, 0) % 2

    def expanded(v):
        n = v.shape[0]
        return jnp.where(own[:n], dot(v[:, :64], e01), 0.0)

    def parents(v, blocks):
        n = len(blocks)
        lhs = jnp.sum(expanded(v).reshape(n, 8, 16, 512), axis=1).astype(BF)
        out = []
        for k in range(n):
            d = dot(jnp.concatenate([lhs[k, :, :256], lhs[k, :, 256:]], axis=0), blocks[k])
            out.append(fold_halves(d[:16], d[16:]).astype(BF))
        return jnp.concatenate(out, axis=0)

    loads[0].wait()
    a = [jnp.where(parity, dot(pick, pt[k]), 0.0).astype(BF) for k in range(GROUPS)]
    x = dot(jnp.concatenate(a, axis=0), fold).astype(BF)
    low = low_lanes((1024, 128))
    xp[...] = jnp.where(low, x[:1024], x[1024:])
    points_ready()
    spread_sources(xd, 128, x)
    wide = expanded(x).astype(BF)
    loads[1].wait()
    coef = []
    for k in range(GROUPS):
        w = wide[128 * k : 128 * (k + 1)]
        c = dot(jnp.concatenate([w[:, :256], w[:, 256:]], axis=0), basis[k])
        coef.append(fold_halves(c[:128], c[128:]).astype(BF))
    coef = jnp.concatenate(coef, axis=0)
    cp[...] = jnp.where(low, coef[:1024], coef[1024:])
    coefs_ready()
    spread_sources(cd, 128, coef)
    loads[2].wait()
    mc[...] = parents(coef, [tl[k] for k in range(GROUPS)])
    loads[3].wait()
    both = parents(mc[...], [tm[0], tm[1]])
    tops[...] = jnp.where(low_lanes((16, 128)), both[:16], both[16:])


def regroup():
    shape = (256, 256)
    row, col = iota(shape, 0), iota(shape, 1)
    return ones_where((row // 32 == col % 8) & (row % 32 == col // 8))


def widen(half):
    shape = (32, 128)
    return ones_where(iota(shape, 1) % 64 == 2 * iota(shape, 0) + half)


def blocks_times(sources, regrouped):
    lhs = jnp.concatenate(sources, axis=1)
    rhs = jnp.concatenate([regrouped[32 * j : 32 * (j + 1)] for j in range(8)], axis=1)
    return dot_nt(lhs, rhs)


def place_messages(cm, mt, mc, msgs, cb):
    rep = iota((8, 8, 128), 2) // 32

    def mid_step(s, carry):
        y = both_halves(mc[pl.ds(pl.multiple_of(s * 16, 16), 16), :])
        y = jnp.concatenate([y] * 4, axis=0)
        zero = jnp.zeros_like(y)
        top = jnp.concatenate([y, zero], axis=1)
        low = jnp.concatenate([zero, y], axis=1)
        block = jnp.concatenate([cm[s, 0:256, :], cm[s, 256:512, :]], axis=1)
        r = dot_nt(block, jnp.concatenate([top, low], axis=0))
        parts = []
        for jh in range(2):
            b = r[:, 128 * jh : 128 * jh + 128].reshape(8, 4, 8, 128)
            q = b[:, 0]
            for k in range(1, 4):
                q = jnp.where(rep == k, b[:, k], q)
            parts.append(q)
        cb[:, pl.ds(pl.multiple_of(s * 16, 16), 16), :] = jnp.concatenate(parts, axis=1).astype(BF)
        return carry

    lax.fori_loop(0, GROUPS, mid_step, 0, unroll=4)

    target = mt[...]
    owner = target // 16
    parts = (owner // 32, (owner // 8) % 4, (owner // 2) % 4, owner % 2, target % 16)
    parts = jnp.concatenate(parts, axis=0).astype(F32).astype(BF)
    shape = (16, 256)
    along = ones_where(iota(shape, 1) % 16 == iota(shape, 0))
    mine = iota(shape, 1) // 16 == iota(shape, 0)
    parts = dot(parts, along)
    y, x, z, c, local = [
        jnp.sum(jnp.where(mine, parts[16 * k : 16 * k + 16], 0.0), axis=0, keepdims=True)
        for k in range(5)
    ]
    shape = (128, 256)
    onehot = iota(shape, 0).astype(F32) == 32.0 * y + 8.0 * x + 2.0 * z + c
    shape = (256, 256)
    earlier = ones_where(iota(shape, 0) < iota(shape, 1))
    rank = jnp.where(onehot, dot(ones_where(onehot), earlier), 0.0)
    rank = jnp.sum(rank, axis=0, keepdims=True)

    plans = (
        (0, 3, 2.0 * x + c, 4.0 * z + y),
        (3, 3, 2.0 * z + c, 4.0 * y + x),
        (6, 2, 2.0 * y + c, 4.0 * x + z),
    )
    for msg, (first, count, stop, rest) in zip(msgs, plans):
        at = 4.0 * rest + rank
        slot = iota((512, 256), 0).astype(F32)
        place = ones_where(slot == 64.0 * stop + at)
        wide = jnp.concatenate([cb[first + k] for k in range(count)], axis=1)
        wide = dot(place, wide).astype(BF)
        for k in range(count):
            rows = wide[:, 128 * k : 128 * k + 128].reshape(8, 64, 128)
            msg[:, 64 * k : 64 * k + 64, :] = rows
        shape = (128, 256)
        to_stop = (iota(shape, 0) // 16).astype(F32) == stop
        value = jnp.where(to_stop, local + 1.0, 0.0).astype(BF)
        lane = ones_where((iota(shape, 0) % 64).astype(F32) == at)
        label = dot_nt(value, lane) - 1.0
        msg[:, 64 * count : 64 * count + 16, :] = label.astype(BF).reshape(8, 16, 128)


def sum_messages(count, landed, sums):
    shape = (16, 128)
    first = iota(shape, 1) < 64
    labels = pl.ds(64 * count, 16)
    lab = [
        jnp.where(first, landed[2 * q, labels, :], landed[2 * q + 1, labels, :])
        for q in range(4)
    ]
    lab = jnp.concatenate(lab, axis=1).astype(F32)
    shape = (16, 512)
    hit = lab == iota(shape, 0).astype(F32)
    to = (iota(shape, 1) // 4) % 16
    lhs = jnp.concatenate([ones_where(hit & (to == n)) for n in range(16)], axis=0)
    parts = [landed[:, 64 * k : 64 * k + 64, :].reshape(512, 128) for k in range(count)]
    total = dot(lhs, jnp.concatenate(parts, axis=1)).astype(BF)
    sums[...] = total.reshape(4, 64, 128 * count)


def near_kernel(
    near_idx, far_idx, ft, mt, near_in, far_in, pt_in, basis_in, tl_in, tm_in, cm_in, tc_in,
    out,
    near, far, near_sum, far_sum, xd, cd, xland, cland, bw, cm, cb, pt, basis, tl, tm, tc, xp, cp, mc, tops,
    all_tops,
    msg_a, msg_b, msg_c, land_a, land_b, land_c,
    sum_a, sum_b, sum_c, next_a, next_b, next_c, part_a, part_b, part_c,
    sums_a, sums_b, sums_c, send, recv, here, fetch,
):
    y = lax.axis_index("grp")
    dev = lax.axis_index("dev")
    x, z, c = dev // 8, (dev // 2) % 4, dev % 2
    me = y * 32 + dev
    right = lax.rem(me + 1, DEVICES)
    left = lax.rem(me + DEVICES - 1, DEVICES)
    mesh = pl.DeviceIdType.MESH

    def remote(src, dst, n, device):
        return pltpu.make_async_remote_copy(
            src_ref=src,
            dst_ref=dst,
            send_sem=send.at[n],
            recv_sem=recv.at[n],
            device_id=device,
            device_id_type=mesh,
        )

    def at_x(k):
        return (y, lax.rem(x + k, 4) * 8 + z * 2 + c)

    def at_y(k):
        return (lax.rem(y + k, 4), dev)

    def at_z(k):
        return (y, x * 8 + lax.rem(z + k, 4) * 2 + c)

    def at_xc(k):
        m = lax.rem(x * 2 + c + k, 8)
        return (y, (m // 2) * 8 + z * 2 + m % 2)

    def at_yc(k):
        m = lax.rem(y * 2 + c + k, 8)
        return (m // 2, x * 8 + z * 2 + m % 2)

    def at_zc(k):
        return (y, x * 8 + lax.rem(z * 2 + c + k, 8))

    def halos(n):
        src, dst = ((xp, xland), (cp, cland))[n]
        return [
            remote(src, dst.at[k], 2 * n + k, (to // 32, to % 32))
            for k, to in enumerate((right, left))
        ]

    def tops_to(n):
        if n == 0:
            return [remote(tops, all_tops.at[c, y, z, x], 3 + k, at_x(k)) for k in range(1, 4)]
        if n == 1:
            block = all_tops.at[c, y, z]
            return [remote(block, block, 6 + k, at_z(k)) for k in range(1, 4)]
        if n == 2:
            block = all_tops.at[c, y]
            return [remote(block, block, 9 + k, at_y(k)) for k in range(1, 4)]
        block = all_tops.at[c]
        return [remote(block, block, 13, (y, x * 8 + z * 2 + 1 - c))]

    plans = (
        (3, (x, z, y), (at_xc, at_z, at_y), msg_a, land_a, sum_a, next_a, part_a, sums_a),
        (3, (z, y, x), (at_zc, at_y, at_x), msg_b, land_b, sum_b, next_b, part_b, sums_b),
        (2, (y, x, z), (at_yc, at_x, at_z), msg_c, land_c, sum_c, next_c, part_c, sums_c),
    )

    def first_hop(n):
        _, (a, _, _), (to, _, _), msg, land = plans[n][:5]
        own = a * 2 + c
        return [
            remote(msg.at[lax.rem(own + k, 8)], land.at[own], 13 + 7 * n + k, to(k))
            for k in range(1, 8)
        ]

    def second_hop(n):
        _, (_, a, _), (_, to, _), _, _, src, dst = plans[n][:7]
        return [
            remote(src.at[lax.rem(a + k, 4)], dst.at[a], 34 + 3 * n + k, to(k))
            for k in range(1, 4)
        ]

    def third_hop(n):
        _, (_, _, a), (_, _, to), _, _, _, _, src, dst = plans[n]
        return [
            remote(src.at[lax.rem(a + k, 4)], dst.at[a], 43 + 3 * n + k, to(k))
            for k in range(1, 4)
        ]

    def own_first(n):
        own = plans[n][1][0] * 2 + c
        return pltpu.make_async_copy(plans[n][3].at[own], plans[n][4].at[own], here.at[n])

    def own_third(n):
        own = plans[n][1][2]
        return pltpu.make_async_copy(plans[n][7].at[own], plans[n][8].at[own], here.at[3 + n])

    def own_tops():
        return pltpu.make_async_copy(tops, all_tops.at[c, y, z, x], here.at[6])

    def chunk(src, dst, base, n):
        part = pl.ds(n * LEAVES, LEAVES)
        return pltpu.make_async_copy(src.at[part], dst.at[part], fetch.at[base + n])

    def start(copies):
        for copy in copies:
            copy.start()

    def arrive(copies):
        for copy in copies:
            copy.wait_recv()

    low = low_lanes((1024, 128))

    def unpack(dst, part, n):
        shape = (128, 128)
        swap = ones_where((iota(shape, 0) + 64) % 128 == iota(shape, 1))
        v = part[...]
        w = dot(v, swap).astype(BF)
        for h, (lo, hi) in enumerate(((v, w), (w, v))):
            at = n * 128 + h * 64
            zero = jnp.zeros_like(v)
            dst[at : at + 64, 0:16, :] = jnp.where(low, lo, zero).reshape(64, 16, 128)
            dst[at : at + 64, 16:32, :] = jnp.where(low, zero, hi).reshape(64, 16, 128)

    pairs = (
        (pt_in, pt), (basis_in, basis), (tl_in, tl), (tm_in, tm), (cm_in, cm), (tc_in, tc),
    )
    loads = [
        pltpu.make_async_copy(src, dst, here.at[7 + n]) for n, (src, dst) in enumerate(pairs)
    ]
    start(loads)
    barrier = pltpu.get_barrier_semaphore()

    def greet(device):
        pl.semaphore_signal(barrier, inc=1, device_id=device, device_id_type=mesh)

    for to in (right, left):
        greet((to // 32, to % 32))
    for k in range(1, 8):
        greet(at_xc(k))
        greet(at_yc(k))
        greet(at_zc(k))

    def points_ready():
        pl.semaphore_wait(barrier, 23)
        start(halos(0))
        start([chunk(near_in, near, 0, n) for n in range(STEPS)])

    def coefs_ready():
        start(halos(1))
        start([chunk(far_in, far, STEPS, n) for n in range(STEPS)])

    up_pass(loads, points_ready, coefs_ready, pt, basis, tl, tm, xp, cp, mc, tops, xd, cd)
    start(tops_to(0))
    own_tops().start()
    loads[4].wait()
    loads[5].wait()
    place_messages(cm, mt, mc, (msg_a, msg_b, msg_c), cb)
    for copies in zip(first_hop(0), first_hop(1), first_hop(2)):
        start(copies)
    for n in range(3):
        own_first(n).start()
    bw[0] = gather_back(0)
    bw[1] = gather_back(1)
    arrive(halos(0))
    unpack(xd, xland.at[0], 0)
    unpack(xd, xland.at[1], 2)

    anchor = (me - 1) * 128

    def work(g, idx, blocks, src, out):
        pair = (iota((32, 256), 1) % 8) // 2
        even = ones_where(iota((1, 16, 128), 1) % 2 == 0)
        odd = ones_where(iota((1, 16, 128), 1) % 2 == 1)
        for i in range(LEAVES):
            found = [src[jnp.clip(idx[j, g * LEAVES + i] - anchor, 0, 383)] for j in range(8)]
            lhs = [jnp.concatenate(found[j : j + 2], axis=1) for j in range(0, 8, 2)]
            block = blocks[g * LEAVES + i].reshape(16, 16, 128)
            rhs = jnp.concatenate([block * even, block * odd], axis=2).reshape(256, 256)
            z = dot_nt(jnp.concatenate(lhs, axis=0), rhs)
            o = z[0:32]
            for j in range(1, 4):
                o = jnp.where(pair == j, z[32 * j : 32 * j + 32], o)
            rows = pl.ds(pl.multiple_of((g * LEAVES + i) * 16, 16), 16)
            out[0, rows, :] = o[:16]
            out[1, rows, :] = o[16:]

    def near_step(g, carry):
        @pl.when(g == 1)
        def _():
            own_tops().wait()
            arrive(tops_to(0))
            start(tops_to(1))

        @pl.when(g == 3)
        def _():
            arrive(tops_to(1))
            start(tops_to(2))

        @pl.when(g == STEPS - 1)
        def _():
            arrive(tops_to(2))
            start(tops_to(3))

        chunk(near_in, near, 0, g).wait()
        work(g, near_idx, near, xd, near_sum)
        return carry

    lax.fori_loop(0, STEPS, near_step, 0)
    for n in range(3):
        own_first(n).wait()
        arrive(first_hop(n))
    arrive(halos(1))
    for n in range(3):
        sum_messages(plans[n][0], plans[n][4], plans[n][5])
    for n in range(3):
        start(second_hop(n))
    unpack(cd, cland.at[0], 0)
    unpack(cd, cland.at[1], 2)

    def far_step(g, carry):
        @pl.when(g == 4)
        def _():
            for n in range(3):
                arrive(second_hop(n))
            for n in range(3):
                at, own, got, dst = plans[n][1][1], plans[n][5], plans[n][6], plans[n][7]
                total = own[at].astype(F32)
                for k in range(1, 4):
                    total = total + got[lax.rem(at + k, 4)].astype(F32)
                dst[...] = total.astype(BF).reshape(dst.shape)
            for n in range(3):
                start(third_hop(n))
                own_third(n).start()

        chunk(far_in, far, STEPS, g).wait()
        work(g, far_idx, far, cd, far_sum)
        return carry

    lax.fori_loop(0, STEPS, far_step, 0)
    arrive(tops_to(3))
    for n in range(3):
        own_third(n).wait()
        arrive(third_hop(n))
    b0, b1 = bw[0], bw[1]
    down = from_tops(ft, all_tops, tc, tm, b0, b1)
    fields = (from_mids((sums_a, sums_b, sums_c)) + down).astype(BF)
    leaves_out(fields, tl, basis, near_sum, far_sum, b0, b1, out)
    sent = [halos(0), halos(1)] + [tops_to(n) for n in range(4)]
    for n in range(3):
        sent += [first_hop(n), second_hop(n), third_hop(n)]
    for copies in sent:
        for copy in copies:
            copy.wait_send()


def converted(first, second, b0, b1):
    first = jnp.concatenate(first, axis=0)
    second = jnp.concatenate(second, axis=0)
    return dot_nt(first, b0) + dot_nt(second, b1)


def for_children(field, t):
    own = own_child()
    d = dot_nt(both_halves(field), t)
    return [
        jnp.where(own, jnp.concatenate([d[16 * k : 16 * k + 16]] * 8, axis=0), 0.0)
        for k in range(2)
    ]


def from_tops(ft, all_tops, tc, tm, b0, b1):
    w0, w1 = widen(0), widen(1)
    order = regroup()
    shape = (128, 128)
    fold = ones_where(iota(shape, 0) % 64 == iota(shape, 1) % 64)
    shape = (16, 128)
    half = iota(shape, 1) // 64
    found = []
    for n in range(32):
        top = ft[n // 16, n % 16]
        dev = top // 2
        y, x, z, c = dev // 32, (dev // 8) % 4, (dev // 2) % 4, dev % 2
        v = all_tops[c, y, z, x]
        found.append(jnp.where(half == top % 2, v, jnp.zeros_like(v)))
    found = dot(jnp.concatenate(found, axis=0), fold).astype(BF)
    fields = []
    for t in range(2):
        total = jnp.zeros((32, 32), F32)
        for jh in range(2):
            regrouped = dot(order, tc[t, jh * 256 : (jh + 1) * 256, :]).astype(BF)
            first = (t * 16 + jh * 8) * 16
            srcs = [both_halves(found[first + 16 * j : first + 16 * (j + 1)]) for j in range(8)]
            total = total + blocks_times(srcs, regrouped)
        total = total.astype(BF)
        fields.append((dot(total[:16], w0) + dot(total[16:], w1)).astype(BF))
    first, second = zip(*[for_children(fields[t], tm[t]) for t in range(2)])
    return converted([v.astype(BF) for v in first], [v.astype(BF) for v in second], b0, b1)


def from_mids(parts):
    wide = []
    for part in parts:
        total = part[0].astype(F32)
        for k in range(1, 4):
            total = total + part[k].astype(F32)
        wide.append(total)
    wide = jnp.concatenate(wide, axis=1).astype(BF)
    shape = (256, 16)
    repeat = ones_where(iota(shape, 0) // 16 == iota(shape, 1))
    shape = (256, 1024)
    keep = iota(shape, 1) % 16 == iota(shape, 0) % 16
    m = jnp.where(keep, dot(repeat, wide), 0.0).astype(BF)
    shape = (1024, 128)
    to_m = ones_where(iota(shape, 0) // 16 == iota(shape, 1) % 64)
    return dot(m, to_m)


def leaves_out(fields, tl, basis, near_sum, far_sum, b0, b1, out):
    own = own_child()
    shape = (64, 128)
    row, col = iota(shape, 0), iota(shape, 1)
    same = row % 8 == col // 16
    pick0 = ones_where(same & (col % 16 == 2 * (row // 8)))
    pick1 = ones_where(same & (col % 16 == 2 * (row // 8) + 1))
    low = low_lanes(shape)
    first, second = [], []
    for k in range(GROUPS):
        m0, m1 = for_children(fields[16 * k : 16 * k + 16], tl[k])
        rows = slice(128 * k, 128 * k + 128)
        first.append((m0 + far_sum[0, rows, :]).astype(BF))
        second.append((m1 + far_sum[1, rows, :]).astype(BF))
    leaf = converted(first, second, b0, b1).astype(BF)
    first, second = [], []
    for k in range(GROUPS):
        rows = slice(128 * k, 128 * k + 128)
        z = dot_nt(both_halves(leaf[rows]), basis[k])
        first.append((jnp.where(own, z[:128], 0.0) + near_sum[0, rows, :]).astype(BF))
        second.append((jnp.where(own, z[128:], 0.0) + near_sum[1, rows, :]).astype(BF))
    total = converted(first, second, b0, b1).astype(BF)
    for k in range(GROUPS):
        v = total[128 * k : 128 * (k + 1)]
        out[k] = jnp.where(low, dot(pick0, v), dot(pick1, v)).astype(BF)


def as_tiles(a):
    n = a.shape[0]
    return a.reshape(n, 8, 32, 128).transpose(0, 2, 1, 3).reshape(n, 256, 128)


VMEM = pl.BlockSpec(memory_space=pltpu.VMEM)
ANY = pl.BlockSpec(memory_space=pl.ANY)
SMEM = pl.BlockSpec(memory_space=pltpu.SMEM)
LIMIT = 56 * 1024 * 1024


def body(
    points,
    basis,
    transfer_leaf,
    transfer_mid,
    near_blocks,
    near_src,
    leaf_coupling,
    far_leaf,
    mid_coupling,
    mid_target,
    top_coupling,
    far_top,
):
    pt = points.reshape(16, 8, 8, 128).transpose(0, 2, 1, 3).reshape(16, 64, 128)
    bt = as_tiles(basis.reshape(16, 8, 4096))
    tl = as_tiles(transfer_leaf.reshape(16, 8, 4096))
    tm = as_tiles(transfer_mid.reshape(2, 8, 4096))
    cm = as_tiles(mid_coupling.reshape(32, 8, 4096)).reshape(16, 512, 128)
    tc = as_tiles(top_coupling.reshape(4, 8, 4096)).reshape(2, 512, 128)
    nb = as_tiles(near_blocks)
    fb = as_tiles(leaf_coupling)

    lanes = (384, 384, 256)
    out = pl.pallas_call(
        near_kernel,
        out_shape=jax.ShapeDtypeStruct((16, 64, 128), BF),
        in_specs=[SMEM] * 3 + [VMEM] + [ANY] * 8,
        out_specs=VMEM,
        scratch_shapes=[
            pltpu.VMEM((128, 256, 128), BF),
            pltpu.VMEM((128, 256, 128), BF),
            pltpu.VMEM((2, 2048, 256), F32),
            pltpu.VMEM((2, 2048, 256), F32),
            pltpu.VMEM((384, 32, 128), BF),
            pltpu.VMEM((384, 32, 128), BF),
            pltpu.VMEM((2, 1024, 128), BF),
            pltpu.VMEM((2, 1024, 128), BF),
            pltpu.VMEM((2, 128, 256), BF),
            pltpu.VMEM((16, 512, 128), BF),
            pltpu.VMEM((8, 256, 128), BF),
            pltpu.VMEM((16, 64, 128), BF),
            pltpu.VMEM((16, 256, 128), BF),
            pltpu.VMEM((16, 256, 128), BF),
            pltpu.VMEM((2, 256, 128), BF),
            pltpu.VMEM((2, 512, 128), BF),
            pltpu.VMEM((1024, 128), BF),
            pltpu.VMEM((1024, 128), BF),
            pltpu.VMEM((256, 128), BF),
            pltpu.VMEM((16, 128), BF),
            pltpu.VMEM((2, 4, 4, 4, 16, 128), BF),
        ]
        + [pltpu.VMEM((8, n // 2 + 16, 128), BF) for n in lanes] * 2
        + [pltpu.VMEM((4, 64, n), BF) for n in lanes] * 2
        + [pltpu.VMEM((4, 16, n), BF) for n in lanes] * 2
        + [
            pltpu.SemaphoreType.DMA((53,)),
            pltpu.SemaphoreType.DMA((53,)),
            pltpu.SemaphoreType.DMA((13,)),
            pltpu.SemaphoreType.DMA((2 * STEPS,)),
        ],
        compiler_params=pltpu.CompilerParams(
            vmem_limit_bytes=LIMIT, collective_id=0, has_side_effects=True
        ),
        name="whole",
    )(near_src.T, far_leaf.T, far_top, mid_target, nb, fb, pt, bt, tl, tm, cm, tc)
    return out.reshape(16, 8, 8, 128).transpose(0, 2, 1, 3).reshape(128, 1024)


def solution(mesh):
    both = P(AXES, None)
    three = P(AXES, None, None)
    return jax.shard_map(
        body,
        mesh=mesh,
        in_specs=(
            both, both, both, both, three, both, three, both, three, both, three, both,
        ),
        out_specs=both,
        check_vma=False,
    )
```

time: 253 us -> 48.1 us (0.19); the launches traced: 250 us -> 48 us
  local copies, waits for them, and re-layouts: 135 us -> 1.67 us
  Pallas kernels: 0 us -> 46.3 us
  blocking collectives: 36.8 us -> 0 us
  matrix products: 36.6 us -> 0 us
  starting transfers between devices: 31.7 us -> 0 us
  other arithmetic: 9.87 us -> 0 us
    reshape x18 -> x0, local copies, waits for them, and re-layouts: 85.6 us -> none  [the longest x1 24 us: body(): near_blocks.reshape(nleaf, NEAR, LEAF, LEAF)]
    pallas_call x0 -> x1, Pallas kernels: none -> 46.3 us  [body(): pl.pallas_call(near_kernel, out_shape=jax.ShapeDtypeStruct((16, 64, 128),...]
    all_gather x1 -> x0, blocking collectives: 36.8 us -> none  [body(): lax.all_gather(top_coef.reshape(ntop, width), ('grp', 'dev'), axis=0, til...]
    dot_general x9 -> x0, matrix products: 36.6 us -> none  [the longest x1 10.8 us: body(): jnp.einsum('irk,ipk->irp', leaf_field, vecs, preferred_element_type=f32)]
    unnamed x21 -> x1, local copies, waits for them, and re-layouts: 27.7 us -> 1.67 us
    all_to_all x2 -> x0, starting transfers between devices: 21.8 us -> none  [the longest x1 15 us: body(): lax.all_to_all(labels.reshape(devices, capacity), ('grp', 'dev'), split_a...]
    gather x4 -> x0, local copies, waits for them, and re-layouts: 11.5 us -> none  [the longest x1 5.36 us: body(): jnp.take(extended, near_src.reshape(-1) - anchor, axis=0)]
    ppermute x4 -> x0, starting transfers between devices: 9.83 us -> none  [the longest x2 7.27 us: extended_2(): before = lax.ppermute(last, axis, up)]
  transfers between devices with their start and end apart: 6 -> 0, of which waited for: 0 -> 0; matrix products, arithmetic and copies ran while one was open for 56% -> 0% of each run, Pallas kernels for 0% -> 0%
where the time goes in v1:
time: 48.1 us; the launch traced here: 48 us
  Pallas kernels  46.3 us (96%)
  local copies, waits for them, and re-layouts  1.67 us (3%)
    pallas_call x1, Pallas kernels, body(): pl.pallas_call(near_kernel, out_shape=jax.ShapeDtypeStruct((16, 64, 128),...  46.3 us
    unnamed x1, local copies, waits for them, and re-layouts  1.67 us

profile of v1, /device:TPU:0, one launch (start us, length us, event | category | flops | bytes accessed | tf_op | source)
XLA Modules:
  0.0 48.0 jit_solution(6728753987112497803)
XLA Ops:
  0.0 46.3 %whole.1 = bf16[16,64,128]{2,1,0:T(8,128)(2,1)} custom-call(s32[8,128]{1,0:T(8,128)} %bitcast.56, s32[8,128]{1,0:T(8,128)} %bitcast.57, s32[2,16]{1,0:T(2,128)} %ft.1, s32[16,16]{1,0:T(8,128)} %mt.1, bf16[128,256,128]{2,1,0:T(8,128)(2,1)} %bitcast.47, bf16[128,256,128]{2,1,0:T(8,128)(2,1)} %bitcast.48, bf16[16,64,128]{2,1,0:T(8,128)(2,1)} %bitcast.53, ...), custom_call_target="tpu_custom_call" | custom-call | tf_op jit(solution)/shard_map/whole/pallas_call | solution.py:609
  46.3 1.7 %copy.14 = bf16[128,1024]{1,0:T(8,128)(2,1)} copy(bf16[128,1024]{1,0:T(8,128)(2,1)} %bitcast.50) | data formatting | bytes 524288

commit v2 on v1

--- a/solution.py
+++ b/solution.py
@@ -62,15 +62,7 @@
     return jnp.concatenate([jnp.where(low, v, zero), jnp.where(low, zero, v)], axis=0)
 
 
-def spread_sources(dst, n, v):
-    low = low_lanes(v.shape)
-    zero = jnp.zeros_like(v)
-    count = v.shape[0] // 16
-    dst[n : n + count, 0:16, :] = jnp.where(low, v, zero).reshape(count, 16, 128)
-    dst[n : n + count, 16:32, :] = jnp.where(low, zero, v).reshape(count, 16, 128)
-
-
-def up_pass(loads, points_ready, coefs_ready, pt, basis, tl, tm, xp, cp, mc, tops, xd, cd):
+def up_pass(loads, points_ready, coefs_ready, pt, basis, tl, tm, xp, cp, mc, tops, xd, cd, own_at):
     e01 = jnp.concatenate([spread(0), spread(1)], axis=1)
     shape = (2048, 512)
     own = (iota(shape, 0) // 16) % 8 == iota(shape, 1) % 8
@@ -102,7 +94,8 @@
     low = low_lanes((1024, 128))
     xp[...] = jnp.where(low, x[:1024], x[1024:])
     points_ready()
-    spread_sources(xd, 128, x)
+    at = pl.ds(pl.multiple_of(own_at, 128), 128)
+    xd[at] = x.reshape(128, 16, 128)
     wide = expanded(x).astype(BF)
     loads[1].wait()
     coef = []
@@ -113,7 +106,7 @@
     coef = jnp.concatenate(coef, axis=0)
     cp[...] = jnp.where(low, coef[:1024], coef[1024:])
     coefs_ready()
-    spread_sources(cd, 128, coef)
+    cd[at] = coef.reshape(128, 16, 128)
     loads[2].wait()
     mc[...] = parents(coef, [tl[k] for k in range(GROUPS)])
     loads[3].wait()
@@ -138,7 +131,7 @@
     return dot_nt(lhs, rhs)
 
 
-def place_messages(cm, mt, mc, msgs, cb):
+def place_messages(cm, mt, mc, msgs, cb, formed):
     rep = iota((8, 8, 128), 2) // 32
 
     def mid_step(s, carry):
@@ -182,10 +175,11 @@
 
     plans = (
         (0, 3, 2.0 * x + c, 4.0 * z + y),
-        (3, 3, 2.0 * z + c, 4.0 * y + x),
-        (6, 2, 2.0 * y + c, 4.0 * x + z),
+        (3, 2, 2.0 * z + c, 4.0 * y + x),
+        (5, 3, 2.0 * y + c, 4.0 * x + z),
     )
-    for msg, (first, count, stop, rest) in zip(msgs, plans):
+    for n, (first, count, stop, rest) in enumerate(plans):
+        msg = msgs[n]
         at = 4.0 * rest + rank
         slot = iota((512, 256), 0).astype(F32)
         place = ones_where(slot == 64.0 * stop + at)
@@ -200,6 +194,7 @@
         lane = ones_where((iota(shape, 0) % 64).astype(F32) == at)
         label = dot_nt(value, lane) - 1.0
         msg[:, 64 * count : 64 * count + 16, :] = label.astype(BF).reshape(8, 16, 128)
+        formed(n)
 
 
 def sum_messages(count, landed, sums):
@@ -223,7 +218,7 @@
 def near_kernel(
     near_idx, far_idx, ft, mt, near_in, far_in, pt_in, basis_in, tl_in, tm_in, cm_in, tc_in,
     out,
-    near, far, near_sum, far_sum, xd, cd, xland, cland, bw, cm, cb, pt, basis, tl, tm, tc, xp, cp, mc, tops,
+    near, far, near_sum, far_sum, near_part, far_part, down, xd, cd, stage, xland, cland, bw, cm, cb, pt, basis, tl, tm, tc, xp, cp, mc, tops,
     all_tops,
     msg_a, msg_b, msg_c, land_a, land_b, land_c,
     sum_a, sum_b, sum_c, next_a, next_b, next_c, part_a, part_b, part_c,
@@ -288,8 +283,8 @@
 
     plans = (
         (3, (x, z, y), (at_xc, at_z, at_y), msg_a, land_a, sum_a, next_a, part_a, sums_a),
-        (3, (z, y, x), (at_zc, at_y, at_x), msg_b, land_b, sum_b, next_b, part_b, sums_b),
-        (2, (y, x, z), (at_yc, at_x, at_z), msg_c, land_c, sum_c, next_c, part_c, sums_c),
+        (2, (z, y, x), (at_zc, at_y, at_x), msg_b, land_b, sum_b, next_b, part_b, sums_b),
+        (3, (y, x, z), (at_yc, at_x, at_z), msg_c, land_c, sum_c, next_c, part_c, sums_c),
     )
 
     def first_hop(n):
@@ -345,10 +340,8 @@
         v = part[...]
         w = dot(v, swap).astype(BF)
         for h, (lo, hi) in enumerate(((v, w), (w, v))):
-            at = n * 128 + h * 64
-            zero = jnp.zeros_like(v)
-            dst[at : at + 64, 0:16, :] = jnp.where(low, lo, zero).reshape(64, 16, 128)
-            dst[at : at + 64, 16:32, :] = jnp.where(low, zero, hi).reshape(64, 16, 128)
+            at = pl.ds(pl.multiple_of((dev + n) % 4 * 128 + h * 64, 64), 64)
+            dst[at] = jnp.where(low, lo, hi).reshape(64, 16, 128)
 
     pairs = (
         (pt_in, pt), (basis_in, basis), (tl_in, tl), (tm_in, tm), (cm_in, cm), (tc_in, tc),
@@ -378,40 +371,43 @@
         start(halos(1))
         start([chunk(far_in, far, STEPS, n) for n in range(STEPS)])
 
-    up_pass(loads, points_ready, coefs_ready, pt, basis, tl, tm, xp, cp, mc, tops, xd, cd)
+    up_pass(loads, points_ready, coefs_ready, pt, basis, tl, tm, xp, cp, mc, tops, xd, cd, dev % 4 * 128)
     start(tops_to(0))
     own_tops().start()
     loads[4].wait()
     loads[5].wait()
-    place_messages(cm, mt, mc, (msg_a, msg_b, msg_c), cb)
-    for copies in zip(first_hop(0), first_hop(1), first_hop(2)):
-        start(copies)
-    for n in range(3):
+
+    def formed(n):
+        start(first_hop(n))
         own_first(n).start()
+
+    place_messages(cm, mt, mc, (msg_a, msg_b, msg_c), cb, formed)
     bw[0] = gather_back(0)
     bw[1] = gather_back(1)
     arrive(halos(0))
-    unpack(xd, xland.at[0], 0)
-    unpack(xd, xland.at[1], 2)
-
-    anchor = (me - 1) * 128
+    unpack(xd, xland.at[0], 3)
+    unpack(xd, xland.at[1], 1)
 
     def work(g, idx, blocks, src, out):
-        pair = (iota((32, 256), 1) % 8) // 2
-        even = ones_where(iota((1, 16, 128), 1) % 2 == 0)
-        odd = ones_where(iota((1, 16, 128), 1) % 2 == 1)
+        low_f = low_lanes((32, 128))
+        low_x = low_lanes((16, 128))
         for i in range(LEAVES):
-            found = [src[jnp.clip(idx[j, g * LEAVES + i] - anchor, 0, 383)] for j in range(8)]
-            lhs = [jnp.concatenate(found[j : j + 2], axis=1) for j in range(0, 8, 2)]
-            block = blocks[g * LEAVES + i].reshape(16, 16, 128)
-            rhs = jnp.concatenate([block * even, block * odd], axis=2).reshape(256, 256)
-            z = dot_nt(jnp.concatenate(lhs, axis=0), rhs)
-            o = z[0:32]
-            for j in range(1, 4):
-                o = jnp.where(pair == j, z[32 * j : 32 * j + 32], o)
-            rows = pl.ds(pl.multiple_of((g * LEAVES + i) * 16, 16), 16)
-            out[0, rows, :] = o[:16]
-            out[1, rows, :] = o[16:]
+            at = g * LEAVES + i
+            plane = stage.at[i]
+            plane[...] = blocks[at].astype(F32)
+            found = [src[idx[j, at] & 511] for j in range(8)]
+            lhs, first, second = [], [], []
+            for j in range(0, 8, 2):
+                lhs.append(jnp.where(low_x, found[j], found[j + 1]))
+                even = plane[pl.ds(j, 32, stride=8), :]
+                odd = plane[pl.ds(j + 1, 32, stride=8), :]
+                turned = pltpu.roll(jnp.where(low_f, odd, even), 64, 1)
+                first.append(jnp.where(low_f, even, turned).astype(BF))
+                second.append(jnp.where(low_f, turned, odd).astype(BF))
+            rhs = [jnp.concatenate(v, axis=1) for v in (first, second)]
+            o = dot_nt(jnp.concatenate(lhs, axis=1), jnp.concatenate(rhs, axis=0))
+            rows = pl.ds(pl.multiple_of(at * 16, 16), 16)
+            out[rows, :] = o
 
     def near_step(g, carry):
         @pl.when(g == 1)
@@ -435,19 +431,22 @@
         return carry
 
     lax.fori_loop(0, STEPS, near_step, 0)
-    for n in range(3):
-        own_first(n).wait()
-        arrive(first_hop(n))
     arrive(halos(1))
-    for n in range(3):
-        sum_messages(plans[n][0], plans[n][4], plans[n][5])
-    for n in range(3):
-        start(second_hop(n))
-    unpack(cd, cland.at[0], 0)
-    unpack(cd, cland.at[1], 2)
+    unpack(cd, cland.at[0], 3)
+    unpack(cd, cland.at[1], 1)
 
     def far_step(g, carry):
-        @pl.when(g == 4)
+        @pl.when(g == 2)
+        def _():
+            for n in range(3):
+                own_first(n).wait()
+                arrive(first_hop(n))
+            for n in range(3):
+                sum_messages(plans[n][0], plans[n][4], plans[n][5])
+            for n in range(3):
+                start(second_hop(n))
+
+        @pl.when(g == STEPS - 1)
         def _():
             for n in range(3):
                 arrive(second_hop(n))
@@ -467,13 +466,18 @@
 
     lax.fori_loop(0, STEPS, far_step, 0)
     arrive(tops_to(3))
+    b0, b1 = bw[0], bw[1]
+    down[...] = from_tops(ft, all_tops, tc, tm, b0, b1)
+    shape = (64, 128)
+    row = iota(shape, 0)
+    in_order = ones_where(iota(shape, 1) % 64 == 2 * (row % 32) + row // 32)
+    near_part[...] = dot(near_sum[...].astype(BF), in_order)
+    far_part[...] = dot(far_sum[...].astype(BF), in_order)
     for n in range(3):
         own_third(n).wait()
         arrive(third_hop(n))
-    b0, b1 = bw[0], bw[1]
-    down = from_tops(ft, all_tops, tc, tm, b0, b1)
-    fields = (from_mids((sums_a, sums_b, sums_c)) + down).astype(BF)
-    leaves_out(fields, tl, basis, near_sum, far_sum, b0, b1, out)
+    fields = (from_mids((sums_a, sums_b, sums_c)) + down[...]).astype(BF)
+    leaves_out(fields, tl, basis, near_part[...], far_part[...], b0, b1, out)
     sent = [halos(0), halos(1)] + [tops_to(n) for n in range(4)]
     for n in range(3):
         sent += [first_hop(n), second_hop(n), third_hop(n)]
@@ -544,7 +548,7 @@
     return dot(m, to_m)
 
 
-def leaves_out(fields, tl, basis, near_sum, far_sum, b0, b1, out):
+def leaves_out(fields, tl, basis, near_part, far_part, b0, b1, out):
     own = own_child()
     shape = (64, 128)
     row, col = iota(shape, 0), iota(shape, 1)
@@ -555,17 +559,15 @@
     first, second = [], []
     for k in range(GROUPS):
         m0, m1 = for_children(fields[16 * k : 16 * k + 16], tl[k])
-        rows = slice(128 * k, 128 * k + 128)
-        first.append((m0 + far_sum[0, rows, :]).astype(BF))
-        second.append((m1 + far_sum[1, rows, :]).astype(BF))
-    leaf = converted(first, second, b0, b1).astype(BF)
+        first.append(m0.astype(BF))
+        second.append(m1.astype(BF))
+    leaf = (converted(first, second, b0, b1) + far_part).astype(BF)
     first, second = [], []
     for k in range(GROUPS):
-        rows = slice(128 * k, 128 * k + 128)
-        z = dot_nt(both_halves(leaf[rows]), basis[k])
-        first.append((jnp.where(own, z[:128], 0.0) + near_sum[0, rows, :]).astype(BF))
-        second.append((jnp.where(own, z[128:], 0.0) + near_sum[1, rows, :]).astype(BF))
-    total = converted(first, second, b0, b1).astype(BF)
+        z = dot_nt(both_halves(leaf[128 * k : 128 * k + 128]), basis[k])
+        first.append(jnp.where(own, z[:128], 0.0).astype(BF))
+        second.append(jnp.where(own, z[128:], 0.0).astype(BF))
+    total = (converted(first, second, b0, b1) + near_part).astype(BF)
     for k in range(GROUPS):
         v = total[128 * k : 128 * (k + 1)]
         out[k] = jnp.where(low, dot(pick0, v), dot(pick1, v)).astype(BF)
@@ -605,7 +607,7 @@
     nb = as_tiles(near_blocks)
     fb = as_tiles(leaf_coupling)
 
-    lanes = (384, 384, 256)
+    lanes = (384, 256, 384)
     out = pl.pallas_call(
         near_kernel,
         out_shape=jax.ShapeDtypeStruct((16, 64, 128), BF),
@@ -614,10 +616,14 @@
         scratch_shapes=[
             pltpu.VMEM((128, 256, 128), BF),
             pltpu.VMEM((128, 256, 128), BF),
-            pltpu.VMEM((2, 2048, 256), F32),
-            pltpu.VMEM((2, 2048, 256), F32),
-            pltpu.VMEM((384, 32, 128), BF),
-            pltpu.VMEM((384, 32, 128), BF),
+            pltpu.VMEM((2048, 64), F32),
+            pltpu.VMEM((2048, 64), F32),
+            pltpu.VMEM((2048, 128), F32),
+            pltpu.VMEM((2048, 128), F32),
+            pltpu.VMEM((256, 128), F32),
+            pltpu.VMEM((512, 16, 128), BF),
+            pltpu.VMEM((512, 16, 128), BF),
+            pltpu.VMEM((LEAVES, 256, 128), F32),
             pltpu.VMEM((2, 1024, 128), BF),
             pltpu.VMEM((2, 1024, 128), BF),
             pltpu.VMEM((2, 128, 256), BF),

time: 48.1 us -> 47.6 us (0.990)
  Pallas kernels: 46.3 us -> 45.8 us
    pallas_call x1, Pallas kernels: 46.3 us -> 45.8 us  [body(): pl.pallas_call(near_kernel, out_shape=jax.ShapeDtypeStruct((16, 64, 128),...]
where the time goes in v2:
time: 47.6 us; the launch traced here: 47.4 us
  Pallas kernels  45.8 us (96%)
  local copies, waits for them, and re-layouts  1.67 us (4%)
    pallas_call x1, Pallas kernels, body(): pl.pallas_call(near_kernel, out_shape=jax.ShapeDtypeStruct((16, 64, 128),...  45.8 us
    unnamed x1, local copies, waits for them, and re-layouts  1.67 us

profile of v2, /device:TPU:0, one launch (start us, length us, event | category | flops | bytes accessed | tf_op | source)
XLA Modules:
  0.0 47.4 jit_solution(18216990159428168362)
XLA Ops:
  0.0 45.8 %whole.1 = bf16[16,64,128]{2,1,0:T(8,128)(2,1)} custom-call(s32[8,128]{1,0:T(8,128)} %bitcast.56, s32[8,128]{1,0:T(8,128)} %bitcast.57, s32[2,16]{1,0:T(2,128)} %ft.1, s32[16,16]{1,0:T(8,128)} %mt.1, bf16[128,256,128]{2,1,0:T(8,128)(2,1)} %bitcast.47, bf16[128,256,128]{2,1,0:T(8,128)(2,1)} %bitcast.48, bf16[16,64,128]{2,1,0:T(8,128)(2,1)} %bitcast.53, ...), custom_call_target="tpu_custom_call" | custom-call | tf_op jit(solution)/shard_map/whole/pallas_call | solution.py:611
  45.8 1.7 %copy.14 = bf16[128,1024]{1,0:T(8,128)(2,1)} copy(bf16[128,1024]{1,0:T(8,128)(2,1)} %bitcast.50) | data formatting | bytes 524288

commit v3 on v2

--- a/solution.py
+++ b/solution.py
@@ -431,22 +431,26 @@
         return carry
 
     lax.fori_loop(0, STEPS, near_step, 0)
+    b0, b1 = bw[0], bw[1]
+    shape = (64, 128)
+    row = iota(shape, 0)
+    in_order = ones_where(iota(shape, 1) % 64 == 2 * (row % 32) + row // 32)
+    for n in range(3):
+        own_first(n).wait()
+        arrive(first_hop(n))
+    for n in range(3):
+        sum_messages(plans[n][0], plans[n][4], plans[n][5])
+    for n in range(3):
+        start(second_hop(n))
+    arrive(tops_to(3))
+    down[...] = from_tops(ft, all_tops, tc, tm, b0, b1)
+    near_part[...] = dot(near_sum[...].astype(BF), in_order)
     arrive(halos(1))
     unpack(cd, cland.at[0], 3)
     unpack(cd, cland.at[1], 1)
 
     def far_step(g, carry):
-        @pl.when(g == 2)
-        def _():
-            for n in range(3):
-                own_first(n).wait()
-                arrive(first_hop(n))
-            for n in range(3):
-                sum_messages(plans[n][0], plans[n][4], plans[n][5])
-            for n in range(3):
-                start(second_hop(n))
-
-        @pl.when(g == STEPS - 1)
+        @pl.when(g == 5)
         def _():
             for n in range(3):
                 arrive(second_hop(n))
@@ -465,13 +469,6 @@
         return carry
 
     lax.fori_loop(0, STEPS, far_step, 0)
-    arrive(tops_to(3))
-    b0, b1 = bw[0], bw[1]
-    down[...] = from_tops(ft, all_tops, tc, tm, b0, b1)
-    shape = (64, 128)
-    row = iota(shape, 0)
-    in_order = ones_where(iota(shape, 1) % 64 == 2 * (row % 32) + row // 32)
-    near_part[...] = dot(near_sum[...].astype(BF), in_order)
     far_part[...] = dot(far_sum[...].astype(BF), in_order)
     for n in range(3):
         own_third(n).wait()
@@ -570,7 +567,7 @@
     total = (converted(first, second, b0, b1) + near_part).astype(BF)
     for k in range(GROUPS):
         v = total[128 * k : 128 * (k + 1)]
-        out[k] = jnp.where(low, dot(pick0, v), dot(pick1, v)).astype(BF)
+        out[k] = jnp.where(low, dot(pick0, v), dot(pick1, v))
 
 
 def as_tiles(a):
@@ -610,7 +607,7 @@
     lanes = (384, 256, 384)
     out = pl.pallas_call(
         near_kernel,
-        out_shape=jax.ShapeDtypeStruct((16, 64, 128), BF),
+        out_shape=jax.ShapeDtypeStruct((16, 64, 128), F32),
         in_specs=[SMEM] * 3 + [VMEM] + [ANY] * 8,
         out_specs=VMEM,
         scratch_shapes=[
@@ -654,7 +651,7 @@
         ),
         name="whole",
     )(near_src.T, far_leaf.T, far_top, mid_target, nb, fb, pt, bt, tl, tm, cm, tc)
-    return out.reshape(16, 8, 8, 128).transpose(0, 2, 1, 3).reshape(128, 1024)
+    return out.astype(BF).reshape(16, 8, 8, 128).transpose(0, 2, 1, 3).reshape(128, 1024)
 
 
 def solution(mesh):

time: 47.6 us -> 47.2 us (level); the launches traced: 47.4 us -> 46.5 us
  other arithmetic: 0 us -> 1.78 us
  local copies, waits for them, and re-layouts: 1.67 us -> 0 us
  Pallas kernels: 45.8 us -> 44.7 us
    reshape x0 -> x1, other arithmetic: none -> 1.78 us  [body(): out.astype(BF).reshape(16, 8, 8, 128).transpose(0, 2, 1, 3)]
    unnamed x1 -> x0, local copies, waits for them, and re-layouts: 1.67 us -> none
    pallas_call x1, Pallas kernels: 45.8 us -> 44.7 us  [body(): pl.pallas_call(near_kernel, out_shape=jax.ShapeDtypeStruct((16, 64, 128),...]
where the time goes in v3:
time: 47.2 us; the launch traced here: 46.5 us
  Pallas kernels  44.7 us (95%)
  other arithmetic  1.78 us (4%)
    pallas_call x1, Pallas kernels, body(): pl.pallas_call(near_kernel, out_shape=jax.ShapeDtypeStruct((16, 64, 128),...  44.7 us
    reshape x1, other arithmetic, body(): out.astype(BF).reshape(16, 8, 8, 128).transpose(0, 2, 1, 3)  1.78 us

profile of v3, /device:TPU:0, one launch (start us, length us, event | category | flops | bytes accessed | tf_op | source)
XLA Modules:
  0.0 46.5 jit_solution(4361369135057976285)
XLA Ops:
  0.0 44.7 %whole.1 = f32[16,64,128]{2,1,0:T(8,128)} custom-call(s32[8,128]{1,0:T(8,128)} %bitcast.56, s32[8,128]{1,0:T(8,128)} %bitcast.57, s32[2,16]{1,0:T(2,128)} %ft.1, s32[16,16]{1,0:T(8,128)} %mt.1, bf16[128,256,128]{2,1,0:T(8,128)(2,1)} %bitcast.48, bf16[128,256,128]{2,1,0:T(8,128)(2,1)} %bitcast.49, bf16[16,64,128]{2,1,0:T(8,128)(2,1)} %bitcast.53, ...), custom_call_target="tpu_custom_call" | custom-call | tf_op jit(solution)/shard_map/whole/pallas_call | solution.py:608
  44.7 1.8 %convert_bitcast_fusion = bf16[128,1024]{1,0:T(8,128)(2,1)} fusion(f32[16,64,128]{2,1,0:T(8,128)} %whole.1), kind=kLoop, calls=%fused_computation | loop fusion | flops 131072 | bytes 786432 | tf_op jit(solution)/shard_map/reshape | solution.py:654

commit v4 on v2

--- a/solution.py
+++ b/solution.py
@@ -416,16 +416,6 @@
             arrive(tops_to(0))
             start(tops_to(1))
 
-        @pl.when(g == 3)
-        def _():
-            arrive(tops_to(1))
-            start(tops_to(2))
-
-        @pl.when(g == STEPS - 1)
-        def _():
-            arrive(tops_to(2))
-            start(tops_to(3))
-
         chunk(near_in, near, 0, g).wait()
         work(g, near_idx, near, xd, near_sum)
         return carry
@@ -445,6 +435,8 @@
                 sum_messages(plans[n][0], plans[n][4], plans[n][5])
             for n in range(3):
                 start(second_hop(n))
+            arrive(tops_to(1))
+            start(tops_to(2))
 
         @pl.when(g == STEPS - 1)
         def _():
@@ -459,20 +451,22 @@
             for n in range(3):
                 start(third_hop(n))
                 own_third(n).start()
+            arrive(tops_to(2))
+            start(tops_to(3))
 
         chunk(far_in, far, STEPS, g).wait()
         work(g, far_idx, far, cd, far_sum)
         return carry
 
     lax.fori_loop(0, STEPS, far_step, 0)
-    arrive(tops_to(3))
     b0, b1 = bw[0], bw[1]
-    down[...] = from_tops(ft, all_tops, tc, tm, b0, b1)
     shape = (64, 128)
     row = iota(shape, 0)
     in_order = ones_where(iota(shape, 1) % 64 == 2 * (row % 32) + row // 32)
     near_part[...] = dot(near_sum[...].astype(BF), in_order)
     far_part[...] = dot(far_sum[...].astype(BF), in_order)
+    arrive(tops_to(3))
+    down[...] = from_tops(ft, all_tops, tc, tm, b0, b1)
     for n in range(3):
         own_third(n).wait()
         arrive(third_hop(n))

time: 47.6 us -> 45 us (0.945); the launches traced: 47.4 us -> 44.2 us
  Pallas kernels: 45.8 us -> 42.5 us
    pallas_call x1, Pallas kernels: 45.8 us -> 42.5 us  [body(): pl.pallas_call(near_kernel, out_shape=jax.ShapeDtypeStruct((16, 64, 128),...]
where the time goes in v4:
time: 45 us; the launch traced here: 44.2 us
  Pallas kernels  42.5 us (94%)
  local copies, waits for them, and re-layouts  1.67 us (4%)
    pallas_call x1, Pallas kernels, body(): pl.pallas_call(near_kernel, out_shape=jax.ShapeDtypeStruct((16, 64, 128),...  42.5 us
    unnamed x1, local copies, waits for them, and re-layouts  1.67 us

profile of v4, /device:TPU:0, one launch (start us, length us, event | category | flops | bytes accessed | tf_op | source)
XLA Modules:
  0.0 44.2 jit_solution(4742653971790759961)
XLA Ops:
  0.0 42.5 %whole.1 = bf16[16,64,128]{2,1,0:T(8,128)(2,1)} custom-call(s32[8,128]{1,0:T(8,128)} %bitcast.56, s32[8,128]{1,0:T(8,128)} %bitcast.57, s32[2,16]{1,0:T(2,128)} %ft.1, s32[16,16]{1,0:T(8,128)} %mt.1, bf16[128,256,128]{2,1,0:T(8,128)(2,1)} %bitcast.47, bf16[128,256,128]{2,1,0:T(8,128)(2,1)} %bitcast.48, bf16[16,64,128]{2,1,0:T(8,128)(2,1)} %bitcast.53, ...), custom_call_target="tpu_custom_call" | custom-call | tf_op jit(solution)/shard_map/whole/pallas_call | solution.py:605
  42.5 1.7 %copy.14 = bf16[128,1024]{1,0:T(8,128)(2,1)} copy(bf16[128,1024]{1,0:T(8,128)(2,1)} %bitcast.50) | data formatting | bytes 524288

commit v5 on v4

--- a/solution.py
+++ b/solution.py
@@ -174,9 +174,9 @@
     rank = jnp.sum(rank, axis=0, keepdims=True)
 
     plans = (
-        (0, 3, 2.0 * x + c, 4.0 * z + y),
-        (3, 2, 2.0 * z + c, 4.0 * y + x),
-        (5, 3, 2.0 * y + c, 4.0 * x + z),
+        (0, 2, 2.0 * x + c, 4.0 * z + y),
+        (2, 2, 2.0 * z + c, 4.0 * y + x),
+        (4, 4, 2.0 * y + c, 4.0 * x + z),
     )
     for n, (first, count, stop, rest) in enumerate(plans):
         msg = msgs[n]
@@ -282,9 +282,9 @@
         return [remote(block, block, 13, (y, x * 8 + z * 2 + 1 - c))]
 
     plans = (
-        (3, (x, z, y), (at_xc, at_z, at_y), msg_a, land_a, sum_a, next_a, part_a, sums_a),
+        (2, (x, z, y), (at_xc, at_z, at_y), msg_a, land_a, sum_a, next_a, part_a, sums_a),
         (2, (z, y, x), (at_zc, at_y, at_x), msg_b, land_b, sum_b, next_b, part_b, sums_b),
-        (3, (y, x, z), (at_yc, at_x, at_z), msg_c, land_c, sum_c, next_c, part_c, sums_c),
+        (4, (y, x, z), (at_yc, at_x, at_z), msg_c, land_c, sum_c, next_c, part_c, sums_c),
     )
 
     def first_hop(n):
@@ -601,7 +601,7 @@
     nb = as_tiles(near_blocks)
     fb = as_tiles(leaf_coupling)
 
-    lanes = (384, 256, 384)
+    lanes = (256, 256, 512)
     out = pl.pallas_call(
         near_kernel,
         out_shape=jax.ShapeDtypeStruct((16, 64, 128), BF),

time: 45 us -> 44.5 us (0.989)
  no operation moved by 1% of the time
where the time goes in v5:
time: 44.5 us; the launch traced here: 43.8 us
  Pallas kernels  42.2 us (95%)
  local copies, waits for them, and re-layouts  1.67 us (4%)
    pallas_call x1, Pallas kernels, body(): pl.pallas_call(near_kernel, out_shape=jax.ShapeDtypeStruct((16, 64, 128),...  42.2 us
    unnamed x1, local copies, waits for them, and re-layouts  1.67 us

profile of v5, /device:TPU:0, one launch (start us, length us, event | category | flops | bytes accessed | tf_op | source)
XLA Modules:
  0.0 43.8 jit_solution(13318559809347954873)
XLA Ops:
  0.0 42.2 %whole.1 = bf16[16,64,128]{2,1,0:T(8,128)(2,1)} custom-call(s32[8,128]{1,0:T(8,128)} %bitcast.56, s32[8,128]{1,0:T(8,128)} %bitcast.57, s32[2,16]{1,0:T(2,128)} %ft.1, s32[16,16]{1,0:T(8,128)} %mt.1, bf16[128,256,128]{2,1,0:T(8,128)(2,1)} %bitcast.47, bf16[128,256,128]{2,1,0:T(8,128)(2,1)} %bitcast.48, bf16[16,64,128]{2,1,0:T(8,128)(2,1)} %bitcast.53, ...), custom_call_target="tpu_custom_call" | custom-call | tf_op jit(solution)/shard_map/whole/pallas_call | solution.py:605
  42.2 1.7 %copy.14 = bf16[128,1024]{1,0:T(8,128)(2,1)} copy(bf16[128,1024]{1,0:T(8,128)(2,1)} %bitcast.50) | data formatting | bytes 524288
